TPU v7x, 32 devices: a whole 2x2x4 slice. The times are simulated.
32 devices in a mesh: groups: 2 (over y), blk: 4 (over z), chan: 2 (over x), pair: 2 (over core).
Axes of the slice: x: 2, y: 2, z: 4, core: 2. Of those that a mesh axis runs over, the one named last changes fastest.
Arguments:
- pair_act: bfloat16 [128, 64, 128], P(('groups', 'blk'), ('chan', 'pair')), parts along dimension 0, may hold values from -6 to 6
- pair_mask: int32 [128, 64], P(('groups', 'blk'), ('chan', 'pair')), parts along dimension 0, may hold values 0 or 1
- in_gain: float32 [128], replicated, may hold values from 0.25 to 1.75
- in_bias: float32 [128], replicated, may hold values from -1.5 to 1.5
- w_proj: bfloat16 [128, 512], replicated, may hold values from -0.5 to 0.5
- w_gate: bfloat16 [128, 128], replicated, may hold values from -0.5 to 0.5
- w_out: bfloat16 [128, 128], replicated, may hold values from -0.5 to 0.5
- out_gain: float32 [128], replicated, may hold values from 0.25 to 1.75
- out_bias: float32 [128], replicated, may hold values from -1.5 to 1.5
Outputs:
- update_cols: bfloat16 [128, 4, 16, 128], P('groups', ('chan', 'pair'), 'blk'), parts along dimension 0
There are 2 independent parts, one for each index of `groups`. A program takes and returns all parts, laid end to end along the dimension named above; an argument that names none is the same for every part. Nothing has to cross between parts.
All inputs are finite; a program needn't handle non-finite values. No bound on the sum of `pair_mask` on one device may be relied on, other than what follows from the above.
Results may differ from a plain program's by a relative error of at most 0.0072.
Values may be sent and summed in bfloat16 or wider, within the bound.
A program may use at most 64 MiB of HBM per device.

v0:
```python
import jax
import jax.numpy as jnp
from jax import lax
from jax.sharding import PartitionSpec as P


def from_behind(value, axis, by):
    count = lax.axis_size(axis)
    return lax.ppermute(value, axis, [(i, (i + by) % count) for i in range(count)])


def norm_axis(values, gain, bias, axis):
    mean = jnp.mean(values, axis=axis, keepdims=True)
    centred = values - mean
    var = jnp.mean(centred * centred, axis=axis, keepdims=True)
    return centred * lax.rsqrt(var + 1e-05) * gain + bias


def on_device(pair_act, pair_mask, in_gain, in_bias, w_proj, w_gate, w_out, out_gain, out_bias):
    rows, cols, width = pair_act.shape
    hidden = w_out.shape[0]
    blocks = lax.axis_size("blk")
    chans = lax.axis_size("chan")
    halves = lax.axis_size("pair")
    normed = norm_axis(pair_act.astype(jnp.float32), in_gain, in_bias, -1).astype(jnp.bfloat16)
    weights = w_proj.reshape(width, 4, hidden)
    proj = jnp.einsum("rkd,dgh->ghrk", normed, weights, preferred_element_type=jnp.float32)
    mask_f = pair_mask.astype(jnp.float32)
    left = (jax.nn.sigmoid(proj[0]) * proj[1] * mask_f).astype(jnp.bfloat16)
    right = (jax.nn.sigmoid(proj[2]) * proj[3] * mask_f).astype(jnp.bfloat16)
    left, right = (
        lax.all_to_all(left, "chan", split_axis=0, concat_axis=2, tiled=True),
        lax.all_to_all(right, "chan", split_axis=0, concat_axis=2, tiled=True),
    )
    subset = left.shape[0]
    me_index = lax.axis_index("blk")
    total = rows * blocks
    zero_index = jnp.zeros((), jnp.int32)

    def place(acc, block, owner):
        part = jnp.einsum("cik,cjk->cij", left, block, preferred_element_type=jnp.float32)
        start = owner * rows
        return lax.dynamic_update_slice(acc, part, (zero_index, zero_index, start))

    acc = jnp.zeros((subset, rows, total), jnp.float32)
    acc = place(acc, right, me_index)

    def both_step(step, carry):
        acc_now, ahead, behind = carry
        ahead = from_behind(ahead, "blk", 1)
        behind = from_behind(behind, "blk", -1)
        acc_now = place(acc_now, ahead, (me_index - step) % blocks)
        acc_now = place(acc_now, behind, (me_index + step) % blocks)
        return (acc_now, ahead, behind)

    acc, ahead, behind = lax.fori_loop(1, (blocks - 1) // 2 + 1, both_step, (acc, right, right))
    ahead = from_behind(ahead, "blk", 1)
    acc = place(acc, ahead, (me_index - blocks // 2) % blocks)
    parts = acc.reshape(subset, rows, chans, halves, cols)
    mine = lax.psum_scatter(parts, "pair", scatter_dimension=3, tiled=True)
    full = lax.all_to_all(mine, "chan", split_axis=2, concat_axis=0, tiled=True)
    full = full.reshape(hidden, rows, cols)
    tri_norm = norm_axis(full, out_gain[:, None, None], out_bias[:, None, None], 0).astype(
        jnp.bfloat16
    )
    linear = jnp.einsum("hrj,hd->rjd", tri_norm, w_out, preferred_element_type=jnp.float32)
    gate = jax.nn.sigmoid(
        jnp.einsum("rjd,de->rje", normed, w_gate, preferred_element_type=jnp.float32)
    )
    update = (gate * linear).astype(jnp.bfloat16).reshape(rows, 1, cols, width)
    return lax.all_to_all(update, "blk", split_axis=2, concat_axis=0, tiled=True)


def solution(mesh):
    return jax.shard_map(
        on_device,
        mesh=mesh,
        in_specs=(
            P(("groups", "blk"), ("chan", "pair"), None),
            P(("groups", "blk"), ("chan", "pair")),
            P(),
            P(),
            P(),
            P(),
            P(),
            P(),
            P(),
        ),
        out_specs=P("groups", ("chan", "pair"), "blk", None),
        check_vma=False,
    )
```

profile of v0, /device:TPU:0, one launch (start us, length us, event | category | flops | bytes accessed | tf_op | source)
XLA Modules:
  0.0 97.3 jit_solution(10640167436970244678)
XLA Ops:
  6.5 0.7 convert_element_type.23
  7.3 0.9 convert_reduce_fusion
  8.2 0.2 fusion.8
  8.5 0.6 copy-done.6
  9.1 0.3 convolution_bitcast_fusion
  9.5 0.4 copy.87
  9.9 1.2 %reshape.69 = bf16[2,2,8192]{2,1,0:T(2,128)(2,1)} reshape(bf16[128,16,16]{2,1,0:T(8,128)(2,1)S(1)} %copy.87) | data formatting | bytes 131072
  11.1 4.2 %all-to-all-start.1 = ((bf16[2,2,8192]{2,1,0:T(2,128)(2,1)}), bf16[2,2,8192]{2,1,0:T(2,128)(2,1)S(1)}, u32[]{:S(2)}, u32[]{:S(2)}) async-start(bf16[2,2,8192]{2,1,0:T(2,128)(2,1)} %reshape.69), calls=%async_computation.1 | async-start | bytes 131072 | tf_op jit(solution)/shard_map/all_to_all | solution.py:33
  15.3 0.4 copy.82
  15.7 1.2 %reshape.67 = bf16[2,2,8192]{2,1,0:T(2,128)(2,1)} reshape(bf16[128,16,16]{2,1,0:T(8,128)(2,1)S(1)} %copy.82) | data formatting | bytes 131072
  16.9 2.5 %all-to-all-done.1 = bf16[2,2,8192]{2,1,0:T(2,128)(2,1)S(1)} async-done(((bf16[2,2,8192]{2,1,0:T(2,128)(2,1)}), bf16[2,2,8192]{2,1,0:T(2,128)(2,1)S(1)}, u32[]{:S(2)}, u32[]{:S(2)}) %all-to-all-start.1) | async-done | bytes 65568 | tf_op jit(solution)/shard_map/all_to_all | solution.py:33
  19.4 3.3 %all-to-all-start = ((bf16[2,2,8192]{2,1,0:T(2,128)(2,1)}), bf16[2,2,8192]{2,1,0:T(2,128)(2,1)S(1)}, u32[]{:S(2)}, u32[]{:S(2)}) async-start(bf16[2,2,8192]{2,1,0:T(2,128)(2,1)} %reshape.67), calls=%async_computation | async-start | bytes 131072 | tf_op jit(solution)/shard_map/all_to_all | solution.py:32
  22.9 0.4 reshape.70
  23.2 0.5 copy.107
  23.7 0.3 copy.91
  24.0 4.2 %collective-permute-start.1 = (bf16[64,16,32]{2,1,0:T(8,128)(2,1)S(1)}, bf16[64,16,32]{2,1,0:T(8,128)(2,1)S(1)}, u32[]{:S(2)}, u32[]{:S(2)}) collective-permute-start(bf16[64,16,32]{2,1,0:T(8,128)(2,1)S(1)} %copy.91), channel_id=1, source_target_pairs={{0,12},{4,0},{8,4},{12,8},{1,13},{5,1},{9,5},{13,9},{2,14},{6,2},{... | collective-permute-start | bytes 196616 | tf_op jit(solution)/shard_map/while/body/eval_jaxpr/ppermute | solution.py:9
  28.2 0.4 reshape.68
  28.6 0.5 copy.106
  29.1 0.3 copy.90
  29.3 0.2 fusion.39
  29.6 0.2 copy.92
  29.9 5.0 %collective-permute-done.1 = bf16[64,16,32]{2,1,0:T(8,128)(2,1)S(1)} collective-permute-done((bf16[64,16,32]{2,1,0:T(8,128)(2,1)S(1)}, bf16[64,16,32]{2,1,0:T(8,128)(2,1)S(1)}, u32[]{:S(2)}, u32[]{:S(2)}) %collective-permute-start.1) | collective-permute-done | bytes 65568 | tf_op jit(solution)/shard_map/while/body/eval_jaxpr/ppermute | solution.py:9
  34.9 0.2 fusion.41
  35.2 0.2 copy.98
  35.4 3.7 %collective-permute-done = bf16[64,16,32]{2,1,0:T(8,128)(2,1)S(1)} collective-permute-done((bf16[64,16,32]{2,1,0:T(8,128)(2,1)S(1)}, bf16[64,16,32]{2,1,0:T(8,128)(2,1)S(1)}, u32[]{:S(2)}, u32[]{:S(2)}) %collective-permute-start) | collective-permute-done | bytes 65568 | tf_op jit(solution)/shard_map/while/body/eval_jaxpr/ppermute | solution.py:9
  39.1 0.2 fusion.40
  39.4 0.2 copy.95
  39.6 1.7 %collective-permute-start.2 = (bf16[64,16,32]{2,1,0:T(8,128)(2,1)S(1)}, bf16[64,16,32]{2,1,0:T(8,128)(2,1)S(1)}, u32[]{:S(2)}, u32[]{:S(2)}) collective-permute-start(bf16[64,16,32]{2,1,0:T(8,128)(2,1)S(1)} %collective-permute-done), channel_id=1, source_target_pairs={{0,4},{4,8},{8,12},{12,0},{1,5},{5,9},{9,13},{13,1},{2,6},{6,10},{... | collective-permute-start | bytes 196616 | tf_op jit(solution)/shard_map/ppermute | solution.py:9
  41.3 6.5 %collective-permute-done.2 = bf16[64,16,32]{2,1,0:T(8,128)(2,1)S(1)} collective-permute-done((bf16[64,16,32]{2,1,0:T(8,128)(2,1)S(1)}, bf16[64,16,32]{2,1,0:T(8,128)(2,1)S(1)}, u32[]{:S(2)}, u32[]{:S(2)}) %collective-permute-start.2) | collective-permute-done | bytes 65568 | tf_op jit(solution)/shard_map/ppermute | solution.py:9
  47.8 0.3 fusion.42
  48.1 0.2 copy.100
  48.4 0.8 copy-done.1
  49.2 0.6 copy-done.9
  49.8 0.6 dynamic-slice
  50.4 16.0 %all-reduce.3.cloned.1.call-done = f32[64,16,2,2,16]{0,4,3,2,1:T(8,128)} async-done(((f32[64,16,2,2,16]{0,4,3,2,1:T(8,128)}), f32[64,16,2,2,16]{0,4,3,2,1:T(8,128)}) %all-reduce.3.cloned.1.call-update) | async-done | bytes 262160
  66.4 1.6 %copy_bitcast_fusion = f32[2,16,1,16,64]{4,3,2,1,0:T(8,128)S(1)} fusion(f32[64,16,2,2,16]{0,4,3,2,1:T(8,128)} %all-reduce.3.cloned.1.call-done, u32[]{:T(128)} %bitcast.28), kind=kLoop, calls=%fused_computation.59 | loop fusion | bytes 393728
  68.2 7.3 %all_to_all.69 = f32[2,1,16384]{2,1,0:T(1,128)S(1)} all-to-all(f32[2,1,16384]{2,1,0:T(1,128)S(1)} %reshape.71), channel_id=1, replica_groups=mesh['groups'=2,'blk'=4,'chan'=2,'pair'=2] {'chan'}, dimensions={0} | all-to-all | bytes 262144 | tf_op jit(solution)/shard_map/all_to_all | solution.py:61
  75.5 0.5 broadcast.69
  76.0 1.0 %reduce.2 = f32[2,16384]{1,0:T(2,128)S(1)} reduce(f32[2,1,16384]{2,1,0:T(1,128)S(1)} %all_to_all.69, f32[]{:T(128)} %broadcast.69), dimensions={1}, to_apply=%all_to_all.58.reduce_sub_computation | reduce | bytes 262148 | tf_op jit(solution)/shard_map/all_to_all | solution.py:61
  77.0 0.2 reshape.72
  77.4 0.2 multiply_reduce_fusion
  77.6 0.2 copy.102
  78.0 0.5 copy-done.3
  78.6 0.2 fusion.29
  78.9 0.5 copy-done.8
  79.4 0.3 fusion.5
  79.7 10.1 %all_to_all.70 = bf16[16,1,16,128]{3,0,1,2:T(8,128)(2,1)S(1)} all-to-all(bf16[16,1,16,128]{3,0,1,2:T(8,128)(2,1)S(1)} %copy.103), channel_id=1, replica_groups=mesh['groups'=2,'blk'=4,'chan'=2,'pair'=2] {'blk'}, dimensions={2} | all-to-all | bytes 131072 | tf_op jit(solution)/shard_map/all_to_all | solution.py:71
  89.8 0.7 copy.104
  (36 shorter events, 1.0 us)
Async XLA Ops:
  6.5 1.9 %copy-start = (bf16[128,512]{1,0:T(8,128)(2,1)S(1)}, bf16[128,512]{1,0:T(8,128)(2,1)}, u32[]{:S(2)}) copy-start(bf16[128,512]{1,0:T(8,128)(2,1)} %param.13) | copy-start | bytes 393220
  6.5 1.7 %copy-start.2 = (bf16[16,16,128]{2,1,0:T(8,128)(2,1)S(1)}, bf16[16,16,128]{2,1,0:T(8,128)(2,1)}, u32[]{:S(2)}) copy-start(bf16[16,16,128]{2,1,0:T(8,128)(2,1)} %param.9) | copy-start | bytes 196612
  8.4 0.7 copy-start.6
  8.5 0.7 copy-start.7
  11.1 8.3 %all-to-all-start.1 = ((bf16[2,2,8192]{2,1,0:T(2,128)(2,1)}), bf16[2,2,8192]{2,1,0:T(2,128)(2,1)S(1)}, u32[]{:S(2)}, u32[]{:S(2)}) async-start(bf16[2,2,8192]{2,1,0:T(2,128)(2,1)} %reshape.69), calls=%async_computation.1 | async-start | bytes 131072 | tf_op jit(solution)/shard_map/all_to_all | solution.py:33
  19.4 8.7 %all-to-all-start = ((bf16[2,2,8192]{2,1,0:T(2,128)(2,1)}), bf16[2,2,8192]{2,1,0:T(2,128)(2,1)S(1)}, u32[]{:S(2)}, u32[]{:S(2)}) async-start(bf16[2,2,8192]{2,1,0:T(2,128)(2,1)} %reshape.67), calls=%async_computation | async-start | bytes 131072 | tf_op jit(solution)/shard_map/all_to_all | solution.py:32
  22.7 43.6 %all-reduce.3.cloned.1.call-start = ((), (), s32[]{:S(2)}) async-start(), calls=%async_computation.4 | async-start | bytes 1048576
  24.0 10.9 %collective-permute-start.1 = (bf16[64,16,32]{2,1,0:T(8,128)(2,1)S(1)}, bf16[64,16,32]{2,1,0:T(8,128)(2,1)S(1)}, u32[]{:S(2)}, u32[]{:S(2)}) collective-permute-start(bf16[64,16,32]{2,1,0:T(8,128)(2,1)S(1)} %copy.91), channel_id=1, source_target_pairs={{0,12},{4,0},{8,4},{12,8},{1,13},{5,1},{9,5},{13,9},{2,14},{6,2},{... | collective-permute-start | bytes 196616 | tf_op jit(solution)/shard_map/while/body/eval_jaxpr/ppermute | solution.py:9
  28.2 10.9 %collective-permute-start = (bf16[64,16,32]{2,1,0:T(8,128)(2,1)S(1)}, bf16[64,16,32]{2,1,0:T(8,128)(2,1)S(1)}, u32[]{:S(2)}, u32[]{:S(2)}) collective-permute-start(bf16[64,16,32]{2,1,0:T(8,128)(2,1)S(1)} %copy.91), channel_id=1, source_target_pairs={{0,4},{4,8},{8,12},{12,0},{1,5},{5,9},{9,13},{13,1},{2,6},{6,10},{... | collective-permute-start | bytes 196616 | tf_op jit(solution)/shard_map/while/body/eval_jaxpr/ppermute | solution.py:9
  39.6 8.2 %collective-permute-start.2 = (bf16[64,16,32]{2,1,0:T(8,128)(2,1)S(1)}, bf16[64,16,32]{2,1,0:T(8,128)(2,1)S(1)}, u32[]{:S(2)}, u32[]{:S(2)}) collective-permute-start(bf16[64,16,32]{2,1,0:T(8,128)(2,1)S(1)} %collective-permute-done), channel_id=1, source_target_pairs={{0,4},{4,8},{8,12},{12,0},{1,5},{5,9},{9,13},{13,1},{2,6},{6,10},{... | collective-permute-start | bytes 196616 | tf_op jit(solution)/shard_map/ppermute | solution.py:9
  48.4 0.8 copy-start.1
  49.2 0.7 copy-start.9
  77.8 0.8 copy-start.3
  78.0 0.7 copy-start.4
  78.0 0.7 copy-start.5
  78.6 0.8 copy-start.8
Sparse Core Ops, SparseCore 0:
  49.3 17.0 all-reduce.2
where the time goes:
time: 98 us; the launch traced here: 97.3 us
  waiting for transfers between devices  33.8 us (34%)
  blocking collectives  17.4 us (18%)
  local copies, waits for them, and re-layouts  13.9 us (14%)
  between operations  13.7 us (14%)
  starting transfers between devices  13.4 us (14%)
  other arithmetic  3.32 us (3%)
  matrix products  1.77 us (2%)
    unnamed x2, waiting for transfers between devices  16 us
    ppermute x3, waiting for transfers between devices, from_behind(): lax.ppermute(value, axis, [(i, (i + by) % count) for i in range(count)])  15.3 us
    all_to_all x1, blocking collectives, on_device(): lax.all_to_all(update, 'blk', split_axis=2, concat_axis=0, tiled=True)  10.1 us
    unnamed x28, local copies, waits for them, and re-layouts  8.91 us
    all_to_all x1, blocking collectives, on_device(): full = lax.all_to_all(mine, 'chan', split_axis=2, concat_axis=0, tiled=True)  7.28 us
    ppermute x3, starting transfers between devices, from_behind(): lax.ppermute(value, axis, [(i, (i + by) % count) for i in range(count)])  5.86 us
    all_to_all x1, starting transfers between devices, on_device(): lax.all_to_all(right, 'chan', split_axis=0, concat_axis=2, tiled=True)  4.21 us
    all_to_all x1, starting transfers between devices, on_device(): lax.all_to_all(left, 'chan', split_axis=0, concat_axis=2, tiled=True)  3.3 us
  transfers between devices with their start and end apart: 6, of which 5 were waited for; matrix products, arithmetic and copies ran while one was open for 6% of the time, Pallas kernels for 0%

commit v1 on v0

--- a/solution.py
+++ b/solution.py
@@ -1,6 +1,10 @@
+import functools
+
 import jax
 import jax.numpy as jnp
 from jax import lax
+from jax.experimental import pallas as pl
+from jax.experimental.pallas import tpu as pltpu
 from jax.sharding import PartitionSpec as P
 
 
@@ -71,21 +75,235 @@
     return lax.all_to_all(update, "blk", split_axis=2, concat_axis=0, tiled=True)
 
 
+MESH = pl.DeviceIdType.MESH
+CELLS = 16
+GROUP = 8
+PIECE = 4
+
+
+def dot(a, b, contract):
+    return lax.dot_general(a, b, ((contract[:1], contract[1:]), ((), ())), preferred_element_type=jnp.float32)
+
+
+def kernel(
+    blocks, chans, halves,
+    act, mask, in_gain, in_bias, w_proj, w_gate, w_out, out_gain, out_bias,
+    out,
+    swap, normed, cells, pick, sides, sides_in, tri_f, tri, tri_in, squares, rows_out,
+    side_send, side_recv, cell_send, cell_recv, tri_send, tri_recv,
+):
+    slabs = chans * halves
+    blk = lax.axis_index("blk")
+    slab = lax.axis_index("chan") * halves + lax.axis_index("pair")
+    me = slab * blocks + blk
+    others = [(ds, db) for db in range(blocks) for ds in range(slabs)]
+
+    def peer(ds, db):
+        s = (slab + ds) % slabs
+        b = (blk + db) % blocks
+        return s, b, s * blocks + b, {"blk": b, "chan": s // halves, "pair": s % halves}
+
+    barrier = pltpu.get_barrier_semaphore()
+    for ds, db in others[1:]:
+        pl.semaphore_signal(barrier, inc=1, device_id=peer(ds, db)[3], device_id_type=MESH)
+
+    x = act[...].astype(jnp.float32)
+    mean = jnp.mean(x, axis=-1, keepdims=True)
+    centred = x - mean
+    var = jnp.mean(centred * centred, axis=-1, keepdims=True)
+    x = centred * lax.rsqrt(var + 1e-05) * in_gain[...].reshape(1, 1, -1) + in_bias[...].reshape(1, 1, -1)
+    for i in range(CELLS):
+        swap[pl.ds(i, CELLS, stride=CELLS), :] = x[i]
+    z = swap[...].astype(jnp.bfloat16)
+    normed[...] = z.reshape(normed.shape)
+
+    lanes = CELLS * CELLS
+    row = lax.broadcasted_iota(jnp.int32, (CELLS, lanes), 0)
+    lane = lax.broadcasted_iota(jnp.int32, (CELLS, lanes), 1)
+    spread = jnp.where(lane // CELLS == row, 1.0, 0.0).astype(jnp.bfloat16)
+    mask_rows = dot(mask[...].astype(jnp.float32).astype(jnp.bfloat16), spread, (1, 0))
+    own_row = lane % CELLS == row
+    mask_row = jnp.sum(jnp.where(own_row, mask_rows, 0.0), axis=0, keepdims=True)
+
+    proj = dot(w_proj[...], z, (0, 1))
+    hidden = proj.shape[0] // 4
+    left = jax.nn.sigmoid(proj[:hidden]) * proj[hidden:2 * hidden] * mask_row
+    right = jax.nn.sigmoid(proj[2 * hidden:3 * hidden]) * proj[3 * hidden:] * mask_row
+    groups = hidden // GROUP
+    both = jnp.concatenate(
+        [left.reshape(groups, GROUP, lanes), right.reshape(groups, GROUP, lanes)], axis=1
+    )
+    sides[...] = both.astype(jnp.bfloat16)
+
+    pl.semaphore_wait(barrier, len(others) - 1)
+    copies = []
+    for n, (ds, db) in list(enumerate(others))[:0:-1]:
+        _, _, to, device = peer(ds, db)
+        copy = pltpu.make_async_remote_copy(
+            src_ref=sides.at[to], dst_ref=sides_in.at[me],
+            send_sem=side_send.at[n], recv_sem=side_recv.at[me],
+            device_id=device, device_id_type=MESH,
+        )
+        copy.start()
+        copies.append(copy)
+    for db in range(1, blocks):
+        b = (blk + db) % blocks
+        copy = pltpu.make_async_remote_copy(
+            src_ref=normed.at[pl.ds(b * PIECE, PIECE)], dst_ref=cells.at[blk],
+            send_sem=cell_send.at[db], recv_sem=cell_recv.at[blk],
+            device_id={"blk": b}, device_id_type=MESH,
+        )
+        copy.start()
+        copies.append(copy)
+    sides_in[me] = sides[me]
+    cells[blk] = normed[pl.ds(blk * PIECE, PIECE)]
+
+    total = slabs * CELLS
+    at = lax.broadcasted_iota(jnp.int32, (lanes, total), 0)
+    col = lax.broadcasted_iota(jnp.int32, (lanes, total), 1)
+    for s in range(slabs):
+        pick[s] = jnp.where(col == at // CELLS + s * CELLS, 1.0, 0.0).astype(jnp.bfloat16)
+    moved = (row % GROUP) // 2 * PIECE + row // GROUP * 2 + row % 2
+    right_row = lane % CELLS == moved
+    gain = jnp.transpose(jnp.broadcast_to(out_gain[...].reshape(1, -1), (hidden, hidden))).reshape(groups, GROUP, hidden)
+    bias = jnp.transpose(jnp.broadcast_to(out_bias[...].reshape(1, -1), (hidden, hidden))).reshape(groups, GROUP, hidden)
+
+    for db in range(blocks):
+        acc = None
+        for ds in range(slabs):
+            s, b, frm, device = peer(ds, db)
+            if (ds, db) != (0, 0):
+                pltpu.make_async_remote_copy(
+                    src_ref=sides.at[frm], dst_ref=sides_in.at[frm],
+                    send_sem=side_send.at[0], recv_sem=side_recv.at[frm],
+                    device_id=device, device_id_type=MESH,
+                ).wait_recv()
+            part = sides_in[frm].astype(jnp.float32)
+            part_left = jnp.where(own_row[None], part[:GROUP][:, None, :], 0.0)
+            part_right = jnp.where(right_row[None], part[GROUP:][:, None, :], 0.0)
+            wide = jnp.concatenate([part_left, part_right], axis=0).reshape(2 * GROUP * CELLS, lanes)
+            term = dot(wide.astype(jnp.bfloat16), pick[s], (1, 0))
+            acc = term if acc is None else acc + term
+        b = (blk + db) % blocks
+        rows_of = pl.ds(pl.multiple_of(b * CELLS, CELLS), CELLS)
+        block = acc.astype(jnp.bfloat16).reshape(2 * GROUP, CELLS, total)
+        squares[:, rows_of, :] = block
+
+    wide_rows = blocks * GROUP
+    for h in range(GROUP):
+        t = dot(squares[GROUP + h], squares[h], (1, 1)).reshape(blocks, 2, GROUP, total)
+        t = jnp.concatenate([t[:, 0], t[:, 1]], axis=-1).reshape(wide_rows, 2 * total)
+        tri_f[pl.ds(h, wide_rows, stride=GROUP), :] = t
+    tri[...] = tri_f[...].astype(jnp.bfloat16).reshape(tri.shape)
+
+    for n, (ds, db) in list(enumerate(others))[:0:-1]:
+        _, _, to, device = peer(ds, db)
+        copy = pltpu.make_async_remote_copy(
+            src_ref=tri.at[to], dst_ref=tri_in.at[me],
+            send_sem=tri_send.at[n], recv_sem=tri_recv.at[me],
+            device_id=device, device_id_type=MESH,
+        )
+        copy.start()
+        copies.append(copy)
+    tri_in[me] = tri[me]
+
+    for db in range(1, blocks):
+        b = (blk + db) % blocks
+        pltpu.make_async_remote_copy(
+            src_ref=cells.at[b], dst_ref=cells.at[b],
+            send_sem=cell_send.at[0], recv_sem=cell_recv.at[b],
+            device_id={"blk": b}, device_id_type=MESH,
+        ).wait_recv()
+    mine = jnp.concatenate([cells[b, m] for m in range(PIECE) for b in range(blocks)], axis=0)
+    gate = jax.nn.sigmoid(dot(mine, w_gate[...], (1, 0)))
+
+    for ds, db in others[1:]:
+        _, _, frm, device = peer(ds, db)
+        pltpu.make_async_remote_copy(
+            src_ref=tri.at[frm], dst_ref=tri_in.at[frm],
+            send_sem=tri_send.at[0], recv_sem=tri_recv.at[frm],
+            device_id=device, device_id_type=MESH,
+        ).wait_recv()
+    full = tri_in[...].astype(jnp.float32).reshape(groups, 2, GROUP, hidden)
+    for q in range(2):
+        t = full[:, q]
+        mean = jnp.mean(t, axis=(0, 1), keepdims=True)
+        centred = t - mean
+        var = jnp.mean(centred * centred, axis=(0, 1), keepdims=True)
+        t = centred * lax.rsqrt(var + 1e-05) * gain + bias
+        linear = dot(t.reshape(hidden, hidden).astype(jnp.bfloat16), w_out[...], (0, 0))
+        for p in range(2):
+            m = p * 2 + q
+            rows_out[pl.ds(m, total, stride=PIECE), :] = linear[p * total:(p + 1) * total] * gate[m * total:(m + 1) * total]
+    out[...] = rows_out[...].astype(jnp.bfloat16)
+    for copy in copies:
+        copy.wait_send()
+
+
+def in_one_kernel(*args):
+    blocks = lax.axis_size("blk")
+    chans = lax.axis_size("chan")
+    halves = lax.axis_size("pair")
+    rows, cols, width = args[0].shape
+    slabs = chans * halves
+    devices = blocks * slabs
+    total = rows * blocks
+    bf16, f32 = jnp.bfloat16, jnp.float32
+    dma = pltpu.SemaphoreType.DMA
+    vmem = pl.BlockSpec(memory_space=pltpu.VMEM)
+    out = pl.pallas_call(
+        functools.partial(kernel, blocks, chans, halves),
+        out_shape=jax.ShapeDtypeStruct((total * PIECE, width), bf16),
+        in_specs=[vmem] * len(args),
+        out_specs=vmem,
+        scratch_shapes=[
+            pltpu.VMEM((rows * cols, width), f32),
+            pltpu.VMEM((cols, rows, width), bf16),
+            pltpu.VMEM((blocks, PIECE, rows, width), bf16),
+            pltpu.VMEM((slabs, rows * cols, total), bf16),
+            pltpu.VMEM((devices, 2 * GROUP, rows * cols), bf16),
+            pltpu.VMEM((devices, 2 * GROUP, rows * cols), bf16),
+            pltpu.VMEM((devices * 2 * GROUP, 2 * total), f32),
+            pltpu.VMEM((devices, 2 * GROUP, 2 * total), bf16),
+            pltpu.VMEM((devices, 2 * GROUP, 2 * total), bf16),
+            pltpu.VMEM((2 * GROUP, total, total), bf16),
+            pltpu.VMEM((total * PIECE, width), f32),
+            dma((devices,)),
+            dma((devices,)),
+            dma((blocks,)),
+            dma((blocks,)),
+            dma((devices,)),
+            dma((devices,)),
+        ],
+        compiler_params=pltpu.CompilerParams(
+            collective_id=0, has_side_effects=True, vmem_limit_bytes=32 * 2**20
+        ),
+    )(*args)
+    return out.reshape(total, 1, PIECE, width)
+
+
+def fits(mesh, act_shape, hidden):
+    groups, blocks, slabs = mesh.shape["groups"], mesh.shape["blk"], mesh.shape["chan"] * mesh.shape["pair"]
+    rows, cols = act_shape[0] // (groups * blocks), act_shape[1] // slabs
+    return (
+        (rows, cols) == (CELLS, CELLS)
+        and act_shape[2] == hidden == 128
+        and blocks * slabs * GROUP == hidden
+        and blocks == slabs == PIECE
+    )
+
+
 def solution(mesh):
-    return jax.shard_map(
-        on_device,
-        mesh=mesh,
-        in_specs=(
-            P(("groups", "blk"), ("chan", "pair"), None),
-            P(("groups", "blk"), ("chan", "pair")),
-            P(),
-            P(),
-            P(),
-            P(),
-            P(),
-            P(),
-            P(),
-        ),
-        out_specs=P("groups", ("chan", "pair"), "blk", None),
-        check_vma=False,
-    )
+    specs = (P(("groups", "blk"), ("chan", "pair"), None), P(("groups", "blk"), ("chan", "pair"))) + (P(),) * 7
+
+    def run(*args):
+        body = in_one_kernel if fits(mesh, args[0].shape, args[6].shape[0]) else on_device
+        return jax.shard_map(
+            body,
+            mesh=mesh,
+            in_specs=specs,
+            out_specs=P("groups", ("chan", "pair"), "blk", None),
+            check_vma=False,
+        )(*args)
+
+    return run

time: 98 us -> 25.1 us (0.26)
  waiting for transfers between devices: 33.8 us -> 0 us
  Pallas kernels: 0 us -> 17.5 us
  blocking collectives: 17.4 us -> 0 us
  between operations: 13.7 us -> 0.02 us
  starting transfers between devices: 13.4 us -> 0 us
  local copies, waits for them, and re-layouts: 13.9 us -> 7.2 us
  other arithmetic: 3.32 us -> 0 us
  matrix products: 1.77 us -> 0 us
    pallas_call x0 -> x1, Pallas kernels: none -> 17.5 us  [in_one_kernel(): pl.pallas_call(functools.partial(kernel, blocks, chans, halves), out_shap...]
    all_to_all x2 -> x0, blocking collectives: 17.4 us -> none  [the longest x1 10.1 us: on_device(): lax.all_to_all(update, 'blk', split_axis=2, concat_axis=0, tiled=True)]
    unnamed x2 -> x0, waiting for transfers between devices: 16 us -> none
    ppermute x3 -> x0, waiting for transfers between devices: 15.3 us -> none  [from_behind(): lax.ppermute(value, axis, [(i, (i + by) % count) for i in range(count)])]
    all_to_all x2 -> x0, starting transfers between devices: 7.5 us -> none  [the longest x1 4.21 us: on_device(): lax.all_to_all(right, 'chan', split_axis=0, concat_axis=2, tiled=True)]
    ppermute x3 -> x0, starting transfers between devices: 5.86 us -> none  [from_behind(): lax.ppermute(value, axis, [(i, (i + by) % count) for i in range(count)])]
    all_to_all x10 -> x0, local copies, waits for them, and re-layouts: 2.88 us -> none  [the longest x3 0.74 us: on_device(): lax.all_to_all(left, 'chan', split_axis=0, concat_axis=2, tiled=True)]
    all_to_all x2 -> x0, waiting for transfers between devices: 2.52 us -> none  [the longest x1 2.52 us: on_device(): lax.all_to_all(right, 'chan', split_axis=0, concat_axis=2, tiled=True)]
  transfers between devices with their start and end apart: 6 -> 0, of which waited for: 5 -> 0; matrix products, arithmetic and copies ran while one was open for 6% -> 0% of each run, Pallas kernels for 0% -> 0%
where the time goes in v1:
time: 25.1 us; the launch traced here: 24.7 us
  Pallas kernels  17.5 us (70%)
  local copies, waits for them, and re-layouts  7.2 us (29%)
    pallas_call x1, Pallas kernels, in_one_kernel(): pl.pallas_call(functools.partial(kernel, blocks, chans, halves), out_shap...  17.5 us
    unnamed x19, local copies, waits for them, and re-layouts  7.2 us

profile of v1, /device:TPU:0, one launch (start us, length us, event | category | flops | bytes accessed | tf_op | source)
XLA Modules:
  0.0 24.7 jit_solution(5835587751145381317)
XLA Ops:
  0.0 0.0 copy-start
  0.0 0.9 %copy-done = bf16[128,512]{1,0:T(8,128)(2,1)S(1)} copy-done((bf16[128,512]{1,0:T(8,128)(2,1)S(1)}, bf16[128,512]{1,0:T(8,128)(2,1)}, u32[]{:S(2)}) %copy-start) | copy-done | bytes 131096
  0.9 0.0 copy-start.1
  0.9 0.8 %copy-done.1 = bf16[16,16,128]{2,1,0:T(8,128)(2,1)S(1)} copy-done((bf16[16,16,128]{2,1,0:T(8,128)(2,1)S(1)}, bf16[16,16,128]{2,1,0:T(8,128)(2,1)}, u32[]{:S(2)}) %copy-start.1) | copy-done | bytes 65560
  1.7 0.0 copy-start.2
  1.7 0.8 %copy-done.2 = bf16[128,128]{1,0:T(8,128)(2,1)S(1)} copy-done((bf16[128,128]{1,0:T(8,128)(2,1)S(1)}, bf16[128,128]{1,0:T(8,128)(2,1)}, u32[]{:S(2)}) %copy-start.2) | copy-done | bytes 32792
  2.5 0.0 copy-start.3
  2.5 0.8 %copy-done.3 = bf16[128,128]{1,0:T(8,128)(2,1)S(1)} copy-done((bf16[128,128]{1,0:T(8,128)(2,1)S(1)}, bf16[128,128]{1,0:T(8,128)(2,1)}, u32[]{:S(2)}) %copy-start.3) | copy-done | bytes 32792
  3.3 0.0 copy-start.4
  3.3 0.7 %copy-done.4 = s32[16,16]{1,0:T(8,128)S(1)} copy-done((s32[16,16]{1,0:T(8,128)S(1)}, s32[16,16]{1,0:T(8,128)}, u32[]{:S(2)}) %copy-start.4) | copy-done | bytes 1048
  4.0 0.0 copy-start.5
  4.0 0.7 %copy-done.5 = f32[128]{0:T(128)S(1)} copy-done((f32[128]{0:T(128)S(1)}, f32[128]{0:T(128)}, u32[]{:S(2)}) %copy-start.5) | copy-done | bytes 536
  4.6 0.0 copy-start.6
  4.6 0.7 %copy-done.6 = f32[128]{0:T(128)S(1)} copy-done((f32[128]{0:T(128)S(1)}, f32[128]{0:T(128)}, u32[]{:S(2)}) %copy-start.6) | copy-done | bytes 536
  5.3 0.0 copy-start.7
  5.3 0.7 %copy-done.7 = f32[128]{0:T(128)S(1)} copy-done((f32[128]{0:T(128)S(1)}, f32[128]{0:T(128)}, u32[]{:S(2)}) %copy-start.7) | copy-done | bytes 536
  5.9 0.0 copy-start.8
  5.9 0.7 %copy-done.8 = f32[128]{0:T(128)S(1)} copy-done((f32[128]{0:T(128)S(1)}, f32[128]{0:T(128)}, u32[]{:S(2)}) %copy-start.8) | copy-done | bytes 536
  6.6 17.5 %shard_map.91 = bf16[256,128]{1,0:T(8,128)(2,1)S(1)} custom-call(bf16[16,16,128]{2,1,0:T(8,128)(2,1)S(1)} %copy-done.1, s32[16,16]{1,0:T(8,128)S(1)} %copy-done.4, f32[128]{0:T(128)S(1)} %copy-done.5, f32[128]{0:T(128)S(1)} %copy-done.6, bf16[128,512]{1,0:T(8,128)(2,1)S(1)} %copy-done, bf16[128,128]{1,0:T(8,128)(2,1)S(1)} %copy-done.2, ...), custom_call_target="tpu_custom_call" | custom-call | tf_op jit(solution)/shard_map/pallas_call | solution.py:254
  24.1 0.6 %copy.12 = bf16[64,1,4,128]{3,2,1,0:T(4,128)(2,1)} copy(bf16[64,1,4,128]{3,2,1,0:T(4,128)(2,1)S(1)} %bitcast.3) | data formatting | bytes 131072
Async XLA Ops:
  0.0 0.9 %copy-start = (bf16[128,512]{1,0:T(8,128)(2,1)S(1)}, bf16[128,512]{1,0:T(8,128)(2,1)}, u32[]{:S(2)}) copy-start(bf16[128,512]{1,0:T(8,128)(2,1)} %w_proj.1) | copy-start | bytes 393220
  0.9 0.8 %copy-start.1 = (bf16[16,16,128]{2,1,0:T(8,128)(2,1)S(1)}, bf16[16,16,128]{2,1,0:T(8,128)(2,1)}, u32[]{:S(2)}) copy-start(bf16[16,16,128]{2,1,0:T(8,128)(2,1)} %act.1) | copy-start | bytes 196612
  1.7 0.8 %copy-start.2 = (bf16[128,128]{1,0:T(8,128)(2,1)S(1)}, bf16[128,128]{1,0:T(8,128)(2,1)}, u32[]{:S(2)}) copy-start(bf16[128,128]{1,0:T(8,128)(2,1)} %w_gate.1) | copy-start | bytes 98308
  2.5 0.8 %copy-start.3 = (bf16[128,128]{1,0:T(8,128)(2,1)S(1)}, bf16[128,128]{1,0:T(8,128)(2,1)}, u32[]{:S(2)}) copy-start(bf16[128,128]{1,0:T(8,128)(2,1)} %w_out.1) | copy-start | bytes 98308
  3.3 0.7 %copy-start.4 = (s32[16,16]{1,0:T(8,128)S(1)}, s32[16,16]{1,0:T(8,128)}, u32[]{:S(2)}) copy-start(s32[16,16]{1,0:T(8,128)} %mask.1) | copy-start | bytes 3076
  4.0 0.7 %copy-start.5 = (f32[128]{0:T(128)S(1)}, f32[128]{0:T(128)}, u32[]{:S(2)}) copy-start(f32[128]{0:T(128)} %in_gain.1) | copy-start | bytes 1540
  4.6 0.7 %copy-start.6 = (f32[128]{0:T(128)S(1)}, f32[128]{0:T(128)}, u32[]{:S(2)}) copy-start(f32[128]{0:T(128)} %in_bias.1) | copy-start | bytes 1540
  5.3 0.7 %copy-start.7 = (f32[128]{0:T(128)S(1)}, f32[128]{0:T(128)}, u32[]{:S(2)}) copy-start(f32[128]{0:T(128)} %out_gain.1) | copy-start | bytes 1540
  5.9 0.7 %copy-start.8 = (f32[128]{0:T(128)S(1)}, f32[128]{0:T(128)}, u32[]{:S(2)}) copy-start(f32[128]{0:T(128)} %out_bias.1) | copy-start | bytes 1540

commit v2 on v1

--- a/solution.py
+++ b/solution.py
@@ -85,13 +85,20 @@
     return lax.dot_general(a, b, ((contract[:1], contract[1:]), ((), ())), preferred_element_type=jnp.float32)
 
 
-def kernel(
-    blocks, chans, halves,
-    act, mask, in_gain, in_bias, w_proj, w_gate, w_out, out_gain, out_bias,
-    out,
-    swap, normed, cells, pick, sides, sides_in, tri_f, tri, tri_in, squares, rows_out,
-    side_send, side_recv, cell_send, cell_recv, tri_send, tri_recv,
-):
+def kernel(blocks, chans, halves, *refs):
+    sources, out, targets = refs[:9], refs[9], refs[10:19]
+    fetched = refs[19]
+    (
+        swap, normed, cells, pick, sides, sides_in, tri_f, tri, tri_in, squares, rows_out,
+        side_send, side_recv, cell_send, cell_recv, tri_send, tri_recv,
+    ) = refs[20:]
+    act, mask, in_gain, in_bias, w_proj, w_gate, w_out, out_gain, out_bias = targets
+    fetches = [
+        pltpu.make_async_copy(source, target, fetched.at[n])
+        for n, (source, target) in enumerate(zip(sources, targets))
+    ]
+    for fetch in fetches:
+        fetch.start()
     slabs = chans * halves
     blk = lax.axis_index("blk")
     slab = lax.axis_index("chan") * halves + lax.axis_index("pair")
@@ -106,6 +113,21 @@
     barrier = pltpu.get_barrier_semaphore()
     for ds, db in others[1:]:
         pl.semaphore_signal(barrier, inc=1, device_id=peer(ds, db)[3], device_id_type=MESH)
+
+    lanes = CELLS * CELLS
+    row = lax.broadcasted_iota(jnp.int32, (CELLS, lanes), 0)
+    lane = lax.broadcasted_iota(jnp.int32, (CELLS, lanes), 1)
+    spread = jnp.where(lane // CELLS == row, 1.0, 0.0).astype(jnp.bfloat16)
+    own_row = lane % CELLS == row
+    total = slabs * CELLS
+    at = lax.broadcasted_iota(jnp.int32, (lanes, total), 0)
+    col = lax.broadcasted_iota(jnp.int32, (lanes, total), 1)
+    for s in range(slabs):
+        pick[s] = jnp.where(col == at // CELLS + s * CELLS, 1.0, 0.0).astype(jnp.bfloat16)
+    moved = (row % GROUP) // 2 * PIECE + row // GROUP * 2 + row % 2
+    right_row = lane % CELLS == moved
+    for fetch in fetches[:4]:
+        fetch.wait()
 
     x = act[...].astype(jnp.float32)
     mean = jnp.mean(x, axis=-1, keepdims=True)
@@ -117,14 +139,10 @@
     z = swap[...].astype(jnp.bfloat16)
     normed[...] = z.reshape(normed.shape)
 
-    lanes = CELLS * CELLS
-    row = lax.broadcasted_iota(jnp.int32, (CELLS, lanes), 0)
-    lane = lax.broadcasted_iota(jnp.int32, (CELLS, lanes), 1)
-    spread = jnp.where(lane // CELLS == row, 1.0, 0.0).astype(jnp.bfloat16)
     mask_rows = dot(mask[...].astype(jnp.float32).astype(jnp.bfloat16), spread, (1, 0))
-    own_row = lane % CELLS == row
     mask_row = jnp.sum(jnp.where(own_row, mask_rows, 0.0), axis=0, keepdims=True)
 
+    fetches[4].wait()
     proj = dot(w_proj[...], z, (0, 1))
     hidden = proj.shape[0] // 4
     left = jax.nn.sigmoid(proj[:hidden]) * proj[hidden:2 * hidden] * mask_row
@@ -158,13 +176,8 @@
     sides_in[me] = sides[me]
     cells[blk] = normed[pl.ds(blk * PIECE, PIECE)]
 
-    total = slabs * CELLS
-    at = lax.broadcasted_iota(jnp.int32, (lanes, total), 0)
-    col = lax.broadcasted_iota(jnp.int32, (lanes, total), 1)
-    for s in range(slabs):
-        pick[s] = jnp.where(col == at // CELLS + s * CELLS, 1.0, 0.0).astype(jnp.bfloat16)
-    moved = (row % GROUP) // 2 * PIECE + row // GROUP * 2 + row % 2
-    right_row = lane % CELLS == moved
+    for fetch in fetches[5:]:
+        fetch.wait()
     gain = jnp.transpose(jnp.broadcast_to(out_gain[...].reshape(1, -1), (hidden, hidden))).reshape(groups, GROUP, hidden)
     bias = jnp.transpose(jnp.broadcast_to(out_bias[...].reshape(1, -1), (hidden, hidden))).reshape(groups, GROUP, hidden)
 
@@ -254,9 +267,10 @@
     out = pl.pallas_call(
         functools.partial(kernel, blocks, chans, halves),
         out_shape=jax.ShapeDtypeStruct((total * PIECE, width), bf16),
-        in_specs=[vmem] * len(args),
+        in_specs=[pl.BlockSpec(memory_space=pltpu.HBM)] * len(args),
         out_specs=vmem,
-        scratch_shapes=[
+        scratch_shapes=[pltpu.VMEM(a.shape, a.dtype) for a in args] + [
+            dma((len(args),)),
             pltpu.VMEM((rows * cols, width), f32),
             pltpu.VMEM((cols, rows, width), bf16),
             pltpu.VMEM((blocks, PIECE, rows, width), bf16),
@@ -276,7 +290,7 @@
             dma((devices,)),
         ],
         compiler_params=pltpu.CompilerParams(
-            collective_id=0, has_side_effects=True, vmem_limit_bytes=32 * 2**20
+            collective_id=0, has_side_effects=True, vmem_limit_bytes=64 * 2**20
         ),
     )(*args)
     return out.reshape(total, 1, PIECE, width)

time: 25.1 us -> 20 us (0.80)
  local copies, waits for them, and re-layouts: 7.2 us -> 1.49 us
  Pallas kernels: 17.5 us -> 18.3 us
    unnamed x19 -> x1, local copies, waits for them, and re-layouts: 7.2 us -> 1.49 us
    pallas_call x1, Pallas kernels: 17.5 us -> 18.3 us  [in_one_kernel(): pl.pallas_call(functools.partial(kernel, blocks, chans, halves), out_shap...]
where the time goes in v2:
time: 20 us; the launch traced here: 19.8 us
  Pallas kernels  18.3 us (92%)
  local copies, waits for them, and re-layouts  1.49 us (7%)
    pallas_call x1, Pallas kernels, in_one_kernel(): pl.pallas_call(functools.partial(kernel, blocks, chans, halves), out_shap...  18.3 us
    unnamed x1, local copies, waits for them, and re-layouts  1.49 us

profile of v2, /device:TPU:0, one launch (start us, length us, event | category | flops | bytes accessed | tf_op | source)
XLA Modules:
  0.0 19.8 jit_solution(5109489340650703329)
XLA Ops:
  0.0 18.3 %shard_map.91 = bf16[256,128]{1,0:T(8,128)(2,1)} custom-call(bf16[16,16,128]{2,1,0:T(8,128)(2,1)} %refs_0_.1, s32[16,16]{1,0:T(8,128)} %refs_1_.1, f32[128]{0:T(128)} %refs_2_.1, f32[128]{0:T(128)} %refs_3_.1, bf16[128,512]{1,0:T(8,128)(2,1)} %refs_4_.1, bf16[128,128]{1,0:T(8,128)(2,1)} %refs_5_.1, bf16[128,128]{1,0:T(8,128)(2,1)} %refs_6_.1, f32[128]{0:T(128)} %refs_7_.1, ...), custom_call_target="tpu_custom_call" | custom-call | tf_op jit(solution)/shard_map/pallas_call | solution.py:267
  18.3 1.5 %copy.12 = bf16[64,1,4,128]{3,2,1,0:T(4,128)(2,1)} copy(bf16[64,1,4,128]{3,2,1,0:T(4,128)(2,1)} %bitcast.3) | data formatting | bytes 131072

commit v3 on v2

--- a/solution.py
+++ b/solution.py
@@ -266,7 +266,7 @@
     vmem = pl.BlockSpec(memory_space=pltpu.VMEM)
     out = pl.pallas_call(
         functools.partial(kernel, blocks, chans, halves),
-        out_shape=jax.ShapeDtypeStruct((total * PIECE, width), bf16),
+        out_shape=pltpu.VMEM((total * PIECE, width), bf16),
         in_specs=[pl.BlockSpec(memory_space=pltpu.HBM)] * len(args),
         out_specs=vmem,
         scratch_shapes=[pltpu.VMEM(a.shape, a.dtype) for a in args] + [
@@ -290,7 +290,7 @@
             dma((devices,)),
         ],
         compiler_params=pltpu.CompilerParams(
-            collective_id=0, has_side_effects=True, vmem_limit_bytes=64 * 2**20
+            collective_id=0, has_side_effects=True, vmem_limit_bytes=60 * 2**20
         ),
     )(*args)
     return out.reshape(total, 1, PIECE, width)

time: 20 us -> 18.4 us (0.920)
  local copies, waits for them, and re-layouts: 1.49 us -> 0.63 us
  Pallas kernels: 18.3 us -> 17.7 us
    unnamed x1, local copies, waits for them, and re-layouts: 1.49 us -> 0.63 us
    pallas_call x1, Pallas kernels: 18.3 us -> 17.7 us  [in_one_kernel(): pl.pallas_call(functools.partial(kernel, blocks, chans, halves), out_shap...]
where the time goes in v3:
time: 18.4 us; the launch traced here: 18.3 us
  Pallas kernels  17.7 us (96%)
  local copies, waits for them, and re-layouts  0.63 us (3%)
    pallas_call x1, Pallas kernels, in_one_kernel(): pl.pallas_call(functools.partial(kernel, blocks, chans, halves), out_shap...  17.7 us
    unnamed x1, local copies, waits for them, and re-layouts  0.63 us

profile of v3, /device:TPU:0, one launch (start us, length us, event | category | flops | bytes accessed | tf_op | source)
XLA Modules:
  0.0 18.3 jit_solution(13473693506427225107)
XLA Ops:
  0.0 17.7 %shard_map.91 = bf16[256,128]{1,0:T(8,128)(2,1)S(1)} custom-call(bf16[16,16,128]{2,1,0:T(8,128)(2,1)} %refs_0_.1, s32[16,16]{1,0:T(8,128)} %refs_1_.1, f32[128]{0:T(128)} %refs_2_.1, f32[128]{0:T(128)} %refs_3_.1, bf16[128,512]{1,0:T(8,128)(2,1)} %refs_4_.1, bf16[128,128]{1,0:T(8,128)(2,1)} %refs_5_.1, bf16[128,128]{1,0:T(8,128)(2,1)} %refs_6_.1, ...), custom_call_target="tpu_custom_call" | custom-call | tf_op jit(solution)/shard_map/pallas_call | solution.py:267
  17.7 0.6 %copy.12 = bf16[64,1,4,128]{3,2,1,0:T(4,128)(2,1)} copy(bf16[64,1,4,128]{3,2,1,0:T(4,128)(2,1)S(1)} %bitcast.3) | data formatting | bytes 131072

commit v4 on v3

--- a/solution.py
+++ b/solution.py
@@ -100,19 +100,24 @@
     for fetch in fetches:
         fetch.start()
     slabs = chans * halves
+    devices = blocks * slabs
     blk = lax.axis_index("blk")
-    slab = lax.axis_index("chan") * halves + lax.axis_index("pair")
+    chan = lax.axis_index("chan")
+    half = lax.axis_index("pair")
+    slab = chan * halves + half
     me = slab * blocks + blk
-    others = [(ds, db) for db in range(blocks) for ds in range(slabs)]
-
-    def peer(ds, db):
-        s = (slab + ds) % slabs
-        b = (blk + db) % blocks
-        return s, b, s * blocks + b, {"blk": b, "chan": s // halves, "pair": s % halves}
+    blks = (blk, blk + 1 - 2 * (blk % 2), (blk + 2) % 4, 3 - blk)
+    chan_of = (chan, 1 - chan)
+    half_of = (half, 1 - half)
+
+    def peer(n):
+        b, c, p = blks[n // 4], chan_of[n // 2 % 2], half_of[n % 2]
+        s = c * halves + p
+        return s, b, s * blocks + b, {"blk": b, "chan": c, "pair": p}
 
     barrier = pltpu.get_barrier_semaphore()
-    for ds, db in others[1:]:
-        pl.semaphore_signal(barrier, inc=1, device_id=peer(ds, db)[3], device_id_type=MESH)
+    for n in range(1, devices):
+        pl.semaphore_signal(barrier, inc=1, device_id=peer(n)[3], device_id_type=MESH)
 
     lanes = CELLS * CELLS
     row = lax.broadcasted_iota(jnp.int32, (CELLS, lanes), 0)
@@ -153,27 +158,27 @@
     )
     sides[...] = both.astype(jnp.bfloat16)
 
-    pl.semaphore_wait(barrier, len(others) - 1)
+    pl.semaphore_wait(barrier, devices - 1)
     copies = []
-    for n, (ds, db) in list(enumerate(others))[:0:-1]:
-        _, _, to, device = peer(ds, db)
+    for n in range(devices - 1, 0, -1):
+        _, _, to, device = peer(n)
         copy = pltpu.make_async_remote_copy(
-            src_ref=sides.at[to], dst_ref=sides_in.at[me],
-            send_sem=side_send.at[n], recv_sem=side_recv.at[me],
+            src_ref=sides.at[to], dst_ref=sides_in.at[n],
+            send_sem=side_send.at[n], recv_sem=side_recv.at[n],
             device_id=device, device_id_type=MESH,
         )
         copy.start()
         copies.append(copy)
-    for db in range(1, blocks):
-        b = (blk + db) % blocks
+    for n in range(1, blocks):
+        b = blks[n]
         copy = pltpu.make_async_remote_copy(
             src_ref=normed.at[pl.ds(b * PIECE, PIECE)], dst_ref=cells.at[blk],
-            send_sem=cell_send.at[db], recv_sem=cell_recv.at[blk],
+            send_sem=cell_send.at[n], recv_sem=cell_recv.at[n],
             device_id={"blk": b}, device_id_type=MESH,
         )
         copy.start()
         copies.append(copy)
-    sides_in[me] = sides[me]
+    sides_in[0] = sides[me]
     cells[blk] = normed[pl.ds(blk * PIECE, PIECE)]
 
     for fetch in fetches[5:]:
@@ -181,23 +186,22 @@
     gain = jnp.transpose(jnp.broadcast_to(out_gain[...].reshape(1, -1), (hidden, hidden))).reshape(groups, GROUP, hidden)
     bias = jnp.transpose(jnp.broadcast_to(out_bias[...].reshape(1, -1), (hidden, hidden))).reshape(groups, GROUP, hidden)
 
-    for db in range(blocks):
+    for nb in range(blocks):
         acc = None
-        for ds in range(slabs):
-            s, b, frm, device = peer(ds, db)
-            if (ds, db) != (0, 0):
+        for n in range(nb * slabs, nb * slabs + slabs):
+            s, b, frm, device = peer(n)
+            if n:
                 pltpu.make_async_remote_copy(
-                    src_ref=sides.at[frm], dst_ref=sides_in.at[frm],
-                    send_sem=side_send.at[0], recv_sem=side_recv.at[frm],
+                    src_ref=sides.at[frm], dst_ref=sides_in.at[n],
+                    send_sem=side_send.at[n], recv_sem=side_recv.at[n],
                     device_id=device, device_id_type=MESH,
                 ).wait_recv()
-            part = sides_in[frm].astype(jnp.float32)
+            part = sides_in[n].astype(jnp.float32)
             part_left = jnp.where(own_row[None], part[:GROUP][:, None, :], 0.0)
             part_right = jnp.where(right_row[None], part[GROUP:][:, None, :], 0.0)
             wide = jnp.concatenate([part_left, part_right], axis=0).reshape(2 * GROUP * CELLS, lanes)
             term = dot(wide.astype(jnp.bfloat16), pick[s], (1, 0))
             acc = term if acc is None else acc + term
-        b = (blk + db) % blocks
         rows_of = pl.ds(pl.multiple_of(b * CELLS, CELLS), CELLS)
         block = acc.astype(jnp.bfloat16).reshape(2 * GROUP, CELLS, total)
         squares[:, rows_of, :] = block
@@ -209,32 +213,32 @@
         tri_f[pl.ds(h, wide_rows, stride=GROUP), :] = t
     tri[...] = tri_f[...].astype(jnp.bfloat16).reshape(tri.shape)
 
-    for n, (ds, db) in list(enumerate(others))[:0:-1]:
-        _, _, to, device = peer(ds, db)
+    for n in range(devices - 1, 0, -1):
+        _, _, to, device = peer(n)
         copy = pltpu.make_async_remote_copy(
             src_ref=tri.at[to], dst_ref=tri_in.at[me],
-            send_sem=tri_send.at[n], recv_sem=tri_recv.at[me],
+            send_sem=tri_send.at[n], recv_sem=tri_recv.at[n],
             device_id=device, device_id_type=MESH,
         )
         copy.start()
         copies.append(copy)
     tri_in[me] = tri[me]
 
-    for db in range(1, blocks):
-        b = (blk + db) % blocks
+    for n in range(1, blocks):
+        b = blks[n]
         pltpu.make_async_remote_copy(
             src_ref=cells.at[b], dst_ref=cells.at[b],
-            send_sem=cell_send.at[0], recv_sem=cell_recv.at[b],
+            send_sem=cell_send.at[n], recv_sem=cell_recv.at[n],
             device_id={"blk": b}, device_id_type=MESH,
         ).wait_recv()
     mine = jnp.concatenate([cells[b, m] for m in range(PIECE) for b in range(blocks)], axis=0)
     gate = jax.nn.sigmoid(dot(mine, w_gate[...], (1, 0)))
 
-    for ds, db in others[1:]:
-        _, _, frm, device = peer(ds, db)
+    for n in range(1, devices):
+        _, _, frm, device = peer(n)
         pltpu.make_async_remote_copy(
             src_ref=tri.at[frm], dst_ref=tri_in.at[frm],
-            send_sem=tri_send.at[0], recv_sem=tri_recv.at[frm],
+            send_sem=tri_send.at[n], recv_sem=tri_recv.at[n],
             device_id=device, device_id_type=MESH,
         ).wait_recv()
     full = tri_in[...].astype(jnp.float32).reshape(groups, 2, GROUP, hidden)
@@ -297,13 +301,14 @@
 
 
 def fits(mesh, act_shape, hidden):
-    groups, blocks, slabs = mesh.shape["groups"], mesh.shape["blk"], mesh.shape["chan"] * mesh.shape["pair"]
+    groups, blocks, chans, halves = (mesh.shape[a] for a in ("groups", "blk", "chan", "pair"))
+    slabs = chans * halves
     rows, cols = act_shape[0] // (groups * blocks), act_shape[1] // slabs
     return (
         (rows, cols) == (CELLS, CELLS)
         and act_shape[2] == hidden == 128
         and blocks * slabs * GROUP == hidden
-        and blocks == slabs == PIECE
+        and (blocks, chans, halves) == (4, 2, 2)
     )
 
 

time: 18.4 us -> 18.6 us (1.011)
  no operation moved by 1% of the time
where the time goes in v4:
time: 18.6 us; the launch traced here: 18.4 us
  Pallas kernels  17.8 us (96%)
  local copies, waits for them, and re-layouts  0.63 us (3%)
    pallas_call x1, Pallas kernels, in_one_kernel(): pl.pallas_call(functools.partial(kernel, blocks, chans, halves), out_shap...  17.8 us
    unnamed x1, local copies, waits for them, and re-layouts  0.63 us

profile of v4, /device:TPU:0, one launch (start us, length us, event | category | flops | bytes accessed | tf_op | source)
XLA Modules:
  0.0 18.4 jit_solution(11171308131701902694)
XLA Ops:
  0.0 17.8 %shard_map.91 = bf16[256,128]{1,0:T(8,128)(2,1)S(1)} custom-call(bf16[16,16,128]{2,1,0:T(8,128)(2,1)} %refs_0_.1, s32[16,16]{1,0:T(8,128)} %refs_1_.1, f32[128]{0:T(128)} %refs_2_.1, f32[128]{0:T(128)} %refs_3_.1, bf16[128,512]{1,0:T(8,128)(2,1)} %refs_4_.1, bf16[128,128]{1,0:T(8,128)(2,1)} %refs_5_.1, bf16[128,128]{1,0:T(8,128)(2,1)} %refs_6_.1, ...), custom_call_target="tpu_custom_call" | custom-call | tf_op jit(solution)/shard_map/pallas_call | solution.py:271
  17.8 0.6 %copy.12 = bf16[64,1,4,128]{3,2,1,0:T(4,128)(2,1)} copy(bf16[64,1,4,128]{3,2,1,0:T(4,128)(2,1)S(1)} %bitcast.3) | data formatting | bytes 131072

commit v5 on v4

--- a/solution.py
+++ b/solution.py
@@ -169,15 +169,6 @@
         )
         copy.start()
         copies.append(copy)
-    for n in range(1, blocks):
-        b = blks[n]
-        copy = pltpu.make_async_remote_copy(
-            src_ref=normed.at[pl.ds(b * PIECE, PIECE)], dst_ref=cells.at[blk],
-            send_sem=cell_send.at[n], recv_sem=cell_recv.at[n],
-            device_id={"blk": b}, device_id_type=MESH,
-        )
-        copy.start()
-        copies.append(copy)
     sides_in[0] = sides[me]
     cells[blk] = normed[pl.ds(blk * PIECE, PIECE)]
 
@@ -186,7 +177,20 @@
     gain = jnp.transpose(jnp.broadcast_to(out_gain[...].reshape(1, -1), (hidden, hidden))).reshape(groups, GROUP, hidden)
     bias = jnp.transpose(jnp.broadcast_to(out_bias[...].reshape(1, -1), (hidden, hidden))).reshape(groups, GROUP, hidden)
 
-    for nb in range(blocks):
+    def send_cells():
+        for n in range(1, blocks):
+            b = blks[n]
+            copy = pltpu.make_async_remote_copy(
+                src_ref=normed.at[pl.ds(b * PIECE, PIECE)], dst_ref=cells.at[blk],
+                send_sem=cell_send.at[n], recv_sem=cell_recv.at[n],
+                device_id={"blk": b}, device_id_type=MESH,
+            )
+            copy.start()
+            copies.append(copy)
+
+    for nb in (0, 1, 3, 2):
+        if nb == 2:
+            send_cells()
         acc = None
         for n in range(nb * slabs, nb * slabs + slabs):
             s, b, frm, device = peer(n)
@@ -223,6 +227,8 @@
         copy.start()
         copies.append(copy)
     tri_in[me] = tri[me]
+    for copy in copies[:1 - devices]:
+        copy.wait_send()
 
     for n in range(1, blocks):
         b = blks[n]
@@ -233,6 +239,8 @@
         ).wait_recv()
     mine = jnp.concatenate([cells[b, m] for m in range(PIECE) for b in range(blocks)], axis=0)
     gate = jax.nn.sigmoid(dot(mine, w_gate[...], (1, 0)))
+    for copy in copies[1 - devices:]:
+        copy.wait_send()
 
     for n in range(1, devices):
         _, _, frm, device = peer(n)
@@ -253,8 +261,6 @@
             m = p * 2 + q
             rows_out[pl.ds(m, total, stride=PIECE), :] = linear[p * total:(p + 1) * total] * gate[m * total:(m + 1) * total]
     out[...] = rows_out[...].astype(jnp.bfloat16)
-    for copy in copies:
-        copy.wait_send()
 
 
 def in_one_kernel(*args):

time: 18.6 us -> 17.6 us (0.946)
  Pallas kernels: 17.8 us -> 16.9 us
    pallas_call x1, Pallas kernels: 17.8 us -> 16.9 us  [in_one_kernel(): pl.pallas_call(functools.partial(kernel, blocks, chans, halves), out_shap...]
where the time goes in v5:
time: 17.6 us; the launch traced here: 17.5 us
  Pallas kernels  16.9 us (96%)
  local copies, waits for them, and re-layouts  0.63 us (4%)
    pallas_call x1, Pallas kernels, in_one_kernel(): pl.pallas_call(functools.partial(kernel, blocks, chans, halves), out_shap...  16.9 us
    unnamed x1, local copies, waits for them, and re-layouts  0.63 us

profile of v5, /device:TPU:0, one launch (start us, length us, event | category | flops | bytes accessed | tf_op | source)
XLA Modules:
  0.0 17.5 jit_solution(8783497614126466358)
XLA Ops:
  0.0 16.9 %shard_map.91 = bf16[256,128]{1,0:T(8,128)(2,1)S(1)} custom-call(bf16[16,16,128]{2,1,0:T(8,128)(2,1)} %refs_0_.1, s32[16,16]{1,0:T(8,128)} %refs_1_.1, f32[128]{0:T(128)} %refs_2_.1, f32[128]{0:T(128)} %refs_3_.1, bf16[128,512]{1,0:T(8,128)(2,1)} %refs_4_.1, bf16[128,128]{1,0:T(8,128)(2,1)} %refs_5_.1, bf16[128,128]{1,0:T(8,128)(2,1)} %refs_6_.1, ...), custom_call_target="tpu_custom_call" | custom-call | tf_op jit(solution)/shard_map/pallas_call | solution.py:277
  16.9 0.6 %copy.12 = bf16[64,1,4,128]{3,2,1,0:T(4,128)(2,1)} copy(bf16[64,1,4,128]{3,2,1,0:T(4,128)(2,1)S(1)} %bitcast.3) | data formatting | bytes 131072

commit v6 on v5

--- a/solution.py
+++ b/solution.py
@@ -189,7 +189,7 @@
             copies.append(copy)
 
     for nb in (0, 1, 3, 2):
-        if nb == 2:
+        if nb == 3:
             send_cells()
         acc = None
         for n in range(nb * slabs, nb * slabs + slabs):

time: 17.6 us -> 17.5 us (level)
  Pallas kernels: 16.9 us -> 16.7 us
    pallas_call x1, Pallas kernels: 16.9 us -> 16.7 us  [in_one_kernel(): pl.pallas_call(functools.partial(kernel, blocks, chans, halves), out_shap...]
where the time goes in v6:
time: 17.5 us; the launch traced here: 17.3 us
  Pallas kernels  16.7 us (95%)
  local copies, waits for them, and re-layouts  0.63 us (4%)
    pallas_call x1, Pallas kernels, in_one_kernel(): pl.pallas_call(functools.partial(kernel, blocks, chans, halves), out_shap...  16.7 us
    unnamed x1, local copies, waits for them, and re-layouts  0.63 us

profile of v6, /device:TPU:0, one launch (start us, length us, event | category | flops | bytes accessed | tf_op | source)
XLA Modules:
  0.0 17.3 jit_solution(4619132976188611937)
XLA Ops:
  0.0 16.7 %shard_map.91 = bf16[256,128]{1,0:T(8,128)(2,1)S(1)} custom-call(bf16[16,16,128]{2,1,0:T(8,128)(2,1)} %refs_0_.1, s32[16,16]{1,0:T(8,128)} %refs_1_.1, f32[128]{0:T(128)} %refs_2_.1, f32[128]{0:T(128)} %refs_3_.1, bf16[128,512]{1,0:T(8,128)(2,1)} %refs_4_.1, bf16[128,128]{1,0:T(8,128)(2,1)} %refs_5_.1, bf16[128,128]{1,0:T(8,128)(2,1)} %refs_6_.1, ...), custom_call_target="tpu_custom_call" | custom-call | tf_op jit(solution)/shard_map/pallas_call | solution.py:277
  16.7 0.6 %copy.12 = bf16[64,1,4,128]{3,2,1,0:T(4,128)(2,1)} copy(bf16[64,1,4,128]{3,2,1,0:T(4,128)(2,1)S(1)} %bitcast.3) | data formatting | bytes 131072
